TPU v7x, 32 devices: a whole 2x2x4 slice. The times are simulated.
32 devices in a mesh: expert: 2 (over x), dp: 16 (over z, y, core).
Axes of the slice: x: 2, y: 2, z: 4, core: 2. Of those that a mesh axis runs over, the one named last changes fastest.
Arguments:
- tokens: bfloat16 [16, 4, 2048], P('dp', 'expert'), may hold values from -6 to 6
- out_grad: bfloat16 [16, 4, 2048], P('dp', 'expert'), may hold values from -6 to 6
- expert_ids: int32 [16, 4, 2], P('dp'), may hold values from 0 to 1, as said below
- gate_scores: bfloat16 [16, 4, 2], P('dp'), may hold values from 0.25 to 1
- w_gate: bfloat16 [2, 2048, 8192], P('expert', None, 'dp'), may hold values from -0.125 to 0.125
- w_up: bfloat16 [2, 2048, 8192], P('expert', None, 'dp'), may hold values from -0.125 to 0.125
- w_down: bfloat16 [2, 8192, 2048], P('expert', 'dp'), may hold values from -0.0625 to 0.0625
Outputs:
- token_grad: bfloat16 [16, 4, 2048], P('dp', 'expert')
- grad_gate: bfloat16 [2, 2048, 8192], P('expert', None, 'dp')
- grad_up: bfloat16 [2, 2048, 8192], P('expert', None, 'dp')
- grad_down: bfloat16 [2, 8192, 2048], P('expert', 'dp')
Inputs may be any that keep to these rules, and one draw needn't show every extreme that they name: `expert_ids`: each token names two different experts; within a group no expert is named by more than 4 tokens, and in every group some expert is named by exactly 4 tokens.
All inputs are finite; a program needn't handle non-finite values.
Results may differ from a plain program's by a relative error of at most 0.0058.
Values may be sent and summed in bfloat16 or wider, within the bound.
No kernel may reach another device: no remote copies, remote signals or barrier semaphores. Data moves between devices by JAX's collectives and lax.ppermute only.
A program may use at most 64 MiB of HBM per device.

v0:
```python
import jax
import jax.numpy as jnp
from jax import lax
from jax.sharding import PartitionSpec as P


def slot_table(expert_ids, experts):
    expert_range = jnp.arange(experts, dtype=jnp.int32)
    naming = jnp.sum((expert_ids[..., :, None] == expert_range).astype(jnp.int32), axis=-2)
    before = jnp.cumsum(naming, axis=-2) - naming
    return jnp.take_along_axis(before, expert_ids, axis=-1)


def local(tokens, out_grad, expert_ids, gate_scores, w_gate, w_up, w_down):
    tok_dev = tokens.shape[1]
    group_tok = expert_ids.shape[1]
    capacity = min(2 * tok_dev + 3, group_tok)
    experts = lax.axis_size("expert")
    my_expert = lax.axis_index("expert")
    group_ids = expert_ids[0]
    group_slots = slot_table(group_ids, experts)
    group_x, group_dy = (
        lax.all_gather(tokens, "expert", axis=1, tiled=True),
        lax.all_gather(out_grad, "expert", axis=1, tiled=True),
    )
    slot_range = jnp.arange(capacity, dtype=jnp.int32)
    matches = (group_ids[None, :, :] == my_expert) & (
        group_slots[None, :, :] == slot_range[:, None, None]
    )
    placing = jnp.sum(matches.astype(jnp.float32), axis=-1)
    weighting = jnp.sum(
        matches.astype(jnp.float32) * gate_scores[0].astype(jnp.float32)[None, :, :], axis=-1
    )
    x_picked = jnp.dot(
        placing.astype(jnp.bfloat16), group_x[0], preferred_element_type=jnp.float32
    ).astype(jnp.bfloat16)
    dy_picked = jnp.dot(
        weighting.astype(jnp.bfloat16), group_dy[0], preferred_element_type=jnp.float32
    ).astype(jnp.bfloat16)
    gate_slab = w_gate[0]
    up_slab = w_up[0]
    down_slab = w_down[0]
    input_rows = lax.all_gather(x_picked, "dp", axis=0, tiled=True)
    pre_gate = jnp.dot(input_rows, gate_slab, preferred_element_type=jnp.float32)
    pre_up = jnp.dot(input_rows, up_slab, preferred_element_type=jnp.float32)
    sigmoid_gate = jax.nn.sigmoid(pre_gate)
    activated = pre_gate * sigmoid_gate
    hidden = (activated * pre_up).astype(jnp.bfloat16)
    grad_rows = lax.all_gather(dy_picked, "dp", axis=0, tiled=True)
    grad_down = jnp.dot(hidden.T, grad_rows, preferred_element_type=jnp.float32).astype(
        jnp.bfloat16
    )
    grad_hidden = jnp.dot(grad_rows, down_slab.T, preferred_element_type=jnp.float32)
    gate_delta = (
        grad_hidden * pre_up * sigmoid_gate * (1.0 + pre_gate * (1.0 - sigmoid_gate))
    ).astype(jnp.bfloat16)
    up_delta = (grad_hidden * activated).astype(jnp.bfloat16)
    grad_gate = jnp.dot(input_rows.T, gate_delta, preferred_element_type=jnp.float32).astype(
        jnp.bfloat16
    )
    grad_up = jnp.dot(input_rows.T, up_delta, preferred_element_type=jnp.float32).astype(
        jnp.bfloat16
    )
    total = jnp.dot(gate_delta, gate_slab.T, preferred_element_type=jnp.float32)
    row_grad = lax.psum_scatter(
        total + jnp.dot(up_delta, up_slab.T, preferred_element_type=jnp.float32),
        "dp",
        scatter_dimension=0,
        tiled=True,
    )
    partial_tokens = jnp.dot(
        placing.T, row_grad, precision=lax.Precision.HIGHEST, preferred_element_type=jnp.float32
    )
    token_grad = lax.psum_scatter(partial_tokens, "expert", scatter_dimension=0, tiled=True)
    return (token_grad.astype(jnp.bfloat16)[None], grad_gate[None], grad_up[None], grad_down[None])


def solution(mesh):
    return jax.shard_map(
        local,
        mesh=mesh,
        in_specs=(
            P("dp", "expert", None),
            P("dp", "expert", None),
            P("dp", None, None),
            P("dp", None, None),
            P("expert", None, "dp"),
            P("expert", None, "dp"),
            P("expert", "dp", None),
        ),
        out_specs=(
            P("dp", "expert", None),
            P("expert", None, "dp"),
            P("expert", None, "dp"),
            P("expert", "dp", None),
        ),
        check_vma=False,
    )
```

profile of v0, /device:TPU:0, one launch (start us, length us, event | category | flops | bytes accessed | tf_op | source)
XLA Modules:
  0.0 174.2 jit_solution(9058850779294097)
XLA Ops:
  7.2 0.0 copy-start
  7.2 0.0 copy-start.3
  7.2 0.0 copy-start.4
  7.2 0.0 all-reduce.4.cloned.1.call-start
  7.2 0.8 fusion.27
  8.1 0.8 copy.53
  8.8 0.7 compare_bitcast_fusion
  9.5 0.7 bitcast_convert_fusion
  10.2 0.7 fusion.24
  10.9 0.1 copy.56
  11.0 0.1 copy.58
  11.1 0.1 reshape.47
  11.2 0.7 gather_fusion
  11.8 0.1 gather.7
  11.9 0.1 copy.59
  12.0 0.0 copy-done.3
  12.1 5.3 %all_gather.14 = bf16[1,4,2048]{2,0,1:T(2,128)(2,1)S(1)} all-gather(bf16[1,2,2048]{2,0,1:T(2,128)(2,1)S(1)} %copy.61), channel_id=1, replica_groups=mesh['expert'=2,'dp'=16] {'expert'}, dimensions={1}, use_global_device_ids=true | all-gather | bytes 24576 | tf_op jit(solution)/shard_map/all_gather | solution.py:23
  17.4 0.0 copy-done.4
  17.4 4.4 %all_gather.12 = bf16[1,4,2048]{2,0,1:T(2,128)(2,1)S(1)} all-gather(bf16[1,2,2048]{2,0,1:T(2,128)(2,1)S(1)} %copy.60), channel_id=1, replica_groups=mesh['expert'=2,'dp'=16] {'expert'}, dimensions={1}, use_global_device_ids=true | all-gather | bytes 24576 | tf_op jit(solution)/shard_map/all_gather | solution.py:24
  21.8 0.1 fusion.3
  22.0 22.9 %all-gather = bf16[16,4,2048]{2,1,0:T(4,128)(2,1)S(1)} all-gather(bf16[1,4,2048]{2,1,0:T(4,128)(2,1)S(1)} %fusion.3), channel_id=1, replica_groups=mesh['expert'=2,'dp'=16] {'dp'}, dimensions={0}, use_global_device_ids=true | all-gather | bytes 278528 | tf_op jit(solution)/shard_map/all_gather | solution.py:49
  44.9 0.1 reshape.55
  44.9 0.1 fusion.4
  45.1 18.2 %all-gather.1 = bf16[16,4,2048]{2,1,0:T(4,128)(2,1)S(1)} all-gather(bf16[1,4,2048]{2,1,0:T(4,128)(2,1)S(1)} %fusion.4), channel_id=1, replica_groups=mesh['expert'=2,'dp'=16] {'dp'}, dimensions={0}, use_global_device_ids=true | all-gather | bytes 278528 | tf_op jit(solution)/shard_map/all_gather | solution.py:43
  63.2 0.1 reshape.57
  63.3 0.0 copy-done
  63.3 0.0 copy-start.1
  63.3 0.0 copy-start.2
  63.3 0.5 fusion.7
  63.8 1.1 copy-done.1
  64.9 0.5 fusion.10
  65.4 0.2 copy-done.2
  65.5 0.8 multiply_convert_fusion.1
  66.3 0.7 fusion.5
  67.1 1.6 convolution_add_fusion
  68.6 0.0 copy-start.6
  68.6 0.0 all-reduce.4.cloned.1.call-update
  68.7 2.1 %fusion.1 = bf16[1,2048,512]{2,1,0:T(8,128)(2,1)} fusion(bf16[64,2048]{1,0:T(8,128)(2,1)S(1)} %reshape.57, bf16[64,512]{1,0:T(8,128)(2,1)S(1)} %get-tuple-element.6), kind=kOutput, calls=%fused_computation.5 | convolution fusion | flops 135266304 | bytes 2424832 | tf_op jit(solution)/shard_map/dot_general | solution.py:61
  70.7 0.0 copy-done.6
  70.7 0.6 dynamic-slice.2
  71.3 0.0 copy-done.5
  71.3 0.6 dynamic-slice
  73.2 2.1 %fusion = bf16[1,2048,512]{2,1,0:T(8,128)(2,1)} fusion(bf16[64,2048]{1,0:T(8,128)(2,1)S(1)} %reshape.57, bf16[64,512]{1,0:T(8,128)(2,1)S(1)} %get-tuple-element.7), kind=kOutput, calls=%fused_computation.4 | convolution fusion | flops 135266304 | bytes 2424832 | tf_op jit(solution)/shard_map/dot_general | solution.py:58
  75.3 2.1 %fusion.2 = bf16[1,512,2048]{2,1,0:T(8,128)(2,1)} fusion(bf16[64,2048]{1,0:T(8,128)(2,1)S(1)} %reshape.55, f32[64,512]{1,0:T(8,128)S(1)} %fusion.10, f32[64,512]{1,0:T(8,128)S(1)} %fusion.7), kind=kOutput, calls=%fused_computation.6 | convolution fusion | flops 135462912 | bytes 2621440 | tf_op jit(solution)/shard_map/dot_general | solution.py:50
  77.3 79.9 %all-reduce.4.cloned.1.call-done = f32[64,2048]{1,0:T(8,128)} async-done(((f32[64,2048]{1,0:T(8,128)}), f32[64,2048]{1,0:T(8,128)}) %all-reduce.4.cloned.1.call-update) | async-done | bytes 524304
  157.3 1.1 fusion.15
  158.4 8.3 %all-reduce.1 = bf16[4,2048]{1,0:T(4,128)(2,1)S(1)} all-reduce(f32[4,2048]{1,0:T(4,128)S(1)} %fusion.15), channel_id=3, replica_groups=mesh['expert'=2,'dp'=16] {'expert'}, use_global_device_ids=true, to_apply=%region_5.6.clone | all-reduce | flops 8192 | bytes 49152
  166.7 0.6 fusion.22
  (7 shorter events, 0.1 us)
Async XLA Ops:
  7.2 56.1 %copy-start = (bf16[1,2048,512]{2,1,0:T(8,128)(2,1)S(1)}, bf16[1,2048,512]{2,1,0:T(8,128)(2,1)}, u32[]{:S(2)}) copy-start(bf16[1,2048,512]{2,1,0:T(8,128)(2,1)} %param.11) | copy-start | bytes 6291460
  7.2 4.9 %copy-start.3 = (bf16[1,2,2048]{2,1,0:T(2,128)(2,1)S(1)}, bf16[1,2,2048]{2,1,0:T(2,128)(2,1)}, u32[]{:S(2)}) copy-start(bf16[1,2,2048]{2,1,0:T(2,128)(2,1)} %param.7) | copy-start | bytes 24580
  7.2 10.2 %copy-start.4 = (bf16[1,2,2048]{2,1,0:T(2,128)(2,1)S(1)}, bf16[1,2,2048]{2,1,0:T(2,128)(2,1)}, u32[]{:S(2)}) copy-start(bf16[1,2,2048]{2,1,0:T(2,128)(2,1)} %param.8) | copy-start | bytes 24580
  7.2 150.1 %all-reduce.4.cloned.1.call-start = ((), (), s32[]{:S(2)}) async-start(), calls=%async_computation | async-start | bytes 1048576
  63.3 1.6 copy-start.1
  63.3 2.2 %copy-start.2 = (bf16[1,512,2048]{2,1,0:T(8,128)(2,1)S(1)}, bf16[1,512,2048]{2,1,0:T(8,128)(2,1)}, u32[]{:S(2)}) copy-start(bf16[1,512,2048]{2,1,0:T(8,128)(2,1)} %param.13) | copy-start | bytes 6291460
  68.6 2.1 %copy-start.6 = (u32[32]{0:T(128)S(1)}, u32[32]{0:T(128)}, u32[]{:S(2)}) copy-start(u32[32]{0:T(128)} %constant.57) | copy-start | bytes 388
  68.6 2.7 %copy-start.5 = (u32[32]{0:T(128)S(1)}, u32[32]{0:T(128)}, u32[]{:S(2)}) copy-start(u32[32]{0:T(128)} %constant.53) | copy-start | bytes 388
Sparse Core Ops, SparseCore 0:
  68.8 88.4 all-reduce.3
where the time goes:
time: 174 us
  waiting for transfers between devices  79.9 us (46%)
  blocking collectives  59.1 us (34%)
  between operations  15.5 us (9%)
  matrix products  11.6 us (7%)
  local copies, waits for them, and re-layouts  5.09 us (3%)
  other arithmetic  2.92 us (2%)
    unnamed x2, waiting for transfers between devices  79.9 us
    all_gather x1, blocking collectives, local(): grad_rows = lax.all_gather(dy_picked, 'dp', axis=0, tiled=True)  22.9 us
    all_gather x1, blocking collectives, local(): input_rows = lax.all_gather(x_picked, 'dp', axis=0, tiled=True)  18.2 us
    unnamed x1, blocking collectives  8.34 us
    all_gather x1, blocking collectives, local(): lax.all_gather(tokens, 'expert', axis=1, tiled=True)  5.31 us
    all_gather x1, blocking collectives, local(): lax.all_gather(out_grad, 'expert', axis=1, tiled=True)  4.42 us
  transfers between devices with their start and end apart: 1, of which 1 were waited for; matrix products, arithmetic and copies ran while one was open for 4% of the time, Pallas kernels for 0%

commit v1 on v0

v1 whole, which is shorter than its diff:
```python
import jax
import jax.numpy as jnp
from jax import lax
from jax.sharding import PartitionSpec as P

LANES = 128
BOTH = ("dp", "expert")


def pack(tokens, out_grad, expert_ids, gate_scores, experts, my_expert):
    tok_dev = tokens.shape[1]
    ids = lax.dynamic_slice_in_dim(expert_ids[0], my_expert * tok_dev, tok_dev, 0)
    scores = lax.dynamic_slice_in_dim(gate_scores[0], my_expert * tok_dev, tok_dev, 0)
    lane = lax.broadcasted_iota(jnp.int32, (tok_dev, LANES), 1)
    table = jnp.zeros((tok_dev, LANES), jnp.bfloat16)
    for k in range(ids.shape[1]):
        table = jnp.where(ids[:, k : k + 1] == lane, scores[:, k : k + 1], table)
    return jnp.concatenate([tokens[0], out_grad[0], table], axis=1)


def local(tokens, out_grad, expert_ids, gate_scores, w_gate, w_up, w_down):
    width = tokens.shape[2]
    tok_dev = tokens.shape[1]
    experts = lax.axis_size("expert")
    devices = experts * lax.axis_size("dp")
    my_expert = lax.axis_index("expert")
    payload = pack(tokens, out_grad, expert_ids, gate_scores, experts, my_expert)
    rows = lax.all_gather(payload, BOTH, axis=0, tiled=True)
    x = rows[:, :width]
    lane = lax.broadcasted_iota(jnp.int32, (rows.shape[0], LANES), 1)
    weight = jnp.sum(
        jnp.where(lane == my_expert, rows[:, 2 * width :].astype(jnp.float32), 0.0),
        axis=1,
        keepdims=True,
    )
    dy = (rows[:, width : 2 * width].astype(jnp.float32) * weight).astype(jnp.bfloat16)
    gate_slab, up_slab, down_slab = w_gate[0], w_up[0], w_down[0]
    pre_gate = jnp.dot(x, gate_slab, preferred_element_type=jnp.float32)
    pre_up = jnp.dot(x, up_slab, preferred_element_type=jnp.float32)
    sigmoid_gate = jax.nn.sigmoid(pre_gate)
    activated = pre_gate * sigmoid_gate
    hidden = (activated * pre_up).astype(jnp.bfloat16)
    grad_hidden = jnp.dot(dy, down_slab.T, preferred_element_type=jnp.float32)
    gate_delta = (
        grad_hidden * pre_up * sigmoid_gate * (1.0 + pre_gate * (1.0 - sigmoid_gate))
    ).astype(jnp.bfloat16)
    up_delta = (grad_hidden * activated).astype(jnp.bfloat16)
    total = jnp.dot(gate_delta, gate_slab.T, preferred_element_type=jnp.float32)
    total = total + jnp.dot(up_delta, up_slab.T, preferred_element_type=jnp.float32)
    shares = total.astype(jnp.bfloat16).reshape(devices, tok_dev, width)
    shares = lax.all_to_all(shares, BOTH, 0, 0, tiled=True)
    token_grad = jnp.sum(shares.astype(jnp.float32), axis=0)
    grad_down = jnp.dot(hidden.T, dy, preferred_element_type=jnp.float32)
    grad_gate = jnp.dot(x.T, gate_delta, preferred_element_type=jnp.float32)
    grad_up = jnp.dot(x.T, up_delta, preferred_element_type=jnp.float32)
    return tuple(g.astype(jnp.bfloat16)[None] for g in (token_grad, grad_gate, grad_up, grad_down))


def solution(mesh):
    return jax.shard_map(
        local,
        mesh=mesh,
        in_specs=(
            P("dp", "expert", None),
            P("dp", "expert", None),
            P("dp", None, None),
            P("dp", None, None),
            P("expert", None, "dp"),
            P("expert", None, "dp"),
            P("expert", "dp", None),
        ),
        out_specs=(
            P("dp", "expert", None),
            P("expert", None, "dp"),
            P("expert", None, "dp"),
            P("expert", "dp", None),
        ),
        check_vma=False,
    )
```

time: 174 us -> 96.6 us (0.56)
  waiting for transfers between devices: 79.9 us -> 4.5 us
  between operations: 15.5 us -> 0.73 us
  blocking collectives: 59.1 us -> 72.8 us
  starting transfers between devices: 0.04 us -> 2.58 us
  matrix products: 11.6 us -> 9.42 us
    unnamed x2 -> x0, waiting for transfers between devices: 79.9 us -> none
    all_gather x4 -> x1, blocking collectives: 50.8 us -> 72.8 us  [local(): rows = lax.all_gather(payload, BOTH, axis=0, tiled=True)]
    unnamed x1 -> x0, blocking collectives: 8.34 us -> none
    all_to_all x0 -> x1, waiting for transfers between devices: none -> 4.5 us  [local(): shares = lax.all_to_all(shares, BOTH, 0, 0, tiled=True)]
    all_to_all x0 -> x1, starting transfers between devices: none -> 2.58 us  [local(): shares = lax.all_to_all(shares, BOTH, 0, 0, tiled=True)]
    unnamed x21 -> x7, local copies, waits for them, and re-layouts: 3.37 us -> 1.38 us
    dynamic_slice x0 -> x4, local copies, waits for them, and re-layouts: none -> 1.83 us  [the longest x2 0.98 us: pack(): lax.dynamic_slice_in_dim(gate_scores[0], my_expert * tok_dev, tok_dev, 0)]
    dot_general x9 -> x6, matrix products: 9.24 us -> 7.91 us  [the longest x1 2.08 us: local(): grad_down = jnp.dot(hidden.T, dy, preferred_element_type=jnp.float32)]
  transfers between devices with their start and end apart: 1 -> 1, of which waited for: 1 -> 1; matrix products, arithmetic and copies ran while one was open for 4% -> 6% of each run, Pallas kernels for 0% -> 0%
where the time goes in v1:
time: 96.6 us; the launch traced here: 96.3 us
  blocking collectives  72.8 us (75%)
  matrix products  9.42 us (10%)
  waiting for transfers between devices  4.5 us (5%)
  local copies, waits for them, and re-layouts  4.46 us (5%)
  starting transfers between devices  2.58 us (3%)
  other arithmetic  1.75 us (2%)
    all_gather x1, blocking collectives, local(): rows = lax.all_gather(payload, BOTH, axis=0, tiled=True)  72.8 us
    all_to_all x1, waiting for transfers between devices, local(): shares = lax.all_to_all(shares, BOTH, 0, 0, tiled=True)  4.5 us
    all_to_all x1, starting transfers between devices, local(): shares = lax.all_to_all(shares, BOTH, 0, 0, tiled=True)  2.58 us
    dot_general x1, matrix products, local(): grad_down = jnp.dot(hidden.T, dy, preferred_element_type=jnp.float32)  2.08 us
    dot_general x1, matrix products, local(): grad_up = jnp.dot(x.T, up_delta, preferred_element_type=jnp.float32)  2.06 us
    dot_general x1, matrix products, local(): grad_gate = jnp.dot(x.T, gate_delta, preferred_element_type=jnp.float32)  2.05 us
  transfers between devices with their start and end apart: 1, of which 1 were waited for; matrix products, arithmetic and copies ran while one was open for 6% of the time, Pallas kernels for 0%

profile of v1, /device:TPU:0, one launch (start us, length us, event | category | flops | bytes accessed | tf_op | source)
XLA Modules:
  0.0 96.3 jit_solution(16922161988926538300)
XLA Ops:
  0.6 0.0 copy-start
  0.7 0.9 constant_dynamic-slice_fusion
  1.5 0.1 copy.16
  1.7 0.7 constant_dynamic-slice_fusion.1
  2.4 0.1 copy.15
  2.5 0.2 slice_reduce_fusion.1
  2.7 0.2 slice_reduce_fusion.2
  2.9 0.1 compare_select_fusion.1
  2.9 0.7 maximum_bitcast_fusion
  3.7 72.8 %all-gather = bf16[32,2,4224]{2,1,0:T(2,128)(2,1)S(1)} all-gather(bf16[1,2,4224]{2,1,0:T(2,128)(2,1)S(1)} %maximum_bitcast_fusion), channel_id=1, replica_groups=mesh['expert'=2,'dp'=16] {'dp','expert'}, dimensions={0}, use_global_device_ids=true | all-gather | bytes 557568 | tf_op jit(solution)/shard_map/all_gather | solution.py:28
  76.5 0.2 reshape.16
  76.7 0.0 copy-start.1
  76.7 0.1 select_reduce_fusion
  76.8 0.0 copy-done
  76.8 0.0 copy-start.2
  76.8 0.5 fusion.6
  77.3 1.0 %copy-done.1 = bf16[1,2048,512]{2,1,0:T(8,128)(2,1)S(1)} copy-done((bf16[1,2048,512]{2,1,0:T(8,128)(2,1)S(1)}, bf16[1,2048,512]{2,1,0:T(8,128)(2,1)}, u32[]{:S(2)}) %copy-start.1) | copy-done | bytes 2097176
  78.3 0.5 fusion.9
  78.8 0.2 copy-done.2
  79.0 0.8 multiply_convert_fusion.2
  79.8 0.7 fusion.4
  80.5 0.8 fusion.3
  81.3 0.9 reshape.14
  82.2 2.6 %all-to-all-start = ((bf16[32,2,2048]{2,1,0:T(2,128)(2,1)}), bf16[32,2,2048]{2,1,0:T(2,128)(2,1)S(1)}, u32[]{:S(2)}, u32[]{:S(2)}) async-start(bf16[32,2,2048]{2,1,0:T(2,128)(2,1)} %reshape.14), calls=%async_computation | async-start | bytes 524288 | tf_op jit(solution)/shard_map/all_to_all | solution.py:51
  84.7 2.1 %fusion.1 = bf16[1,2048,512]{2,1,0:T(8,128)(2,1)} fusion(bf16[64,512]{1,0:T(8,128)(2,1)S(1)} %get-tuple-element.8, bf16[64,4224]{1,0:T(8,128)(2,1)S(1)} %reshape.16), kind=kOutput, calls=%fused_computation.4 | convolution fusion | flops 135266304 | bytes 2424832 | tf_op jit(solution)/shard_map/dot_general | solution.py:55
  86.8 2.1 %fusion = bf16[1,2048,512]{2,1,0:T(8,128)(2,1)} fusion(bf16[64,512]{1,0:T(8,128)(2,1)S(1)} %get-tuple-element.9, bf16[64,4224]{1,0:T(8,128)(2,1)S(1)} %reshape.16), kind=kOutput, calls=%fused_computation.3 | convolution fusion | flops 135266304 | bytes 2424832 | tf_op jit(solution)/shard_map/dot_general | solution.py:54
  88.9 2.1 %fusion.2 = bf16[1,512,2048]{2,1,0:T(8,128)(2,1)} fusion(bf16[64,4224]{1,0:T(8,128)(2,1)S(1)} %reshape.16, f32[64]{0:T(128)S(1)} %select_reduce_fusion, f32[64,512]{1,0:T(8,128)S(1)} %fusion.9, f32[64,512]{1,0:T(8,128)S(1)} %fusion.6), kind=kOutput, calls=%fused_computation.5 | convolution fusion | flops 135856128 | bytes 2621952 | tf_op jit(solution)/shard_map/dot_general | solution.py:53
  90.9 4.5 %all-to-all-done = bf16[32,2,2048]{2,1,0:T(2,128)(2,1)S(1)} async-done(((bf16[32,2,2048]{2,1,0:T(2,128)(2,1)}), bf16[32,2,2048]{2,1,0:T(2,128)(2,1)S(1)}, u32[]{:S(2)}, u32[]{:S(2)}) %all-to-all-start) | async-done | bytes 262176 | tf_op jit(solution)/shard_map/all_to_all | solution.py:51
  95.4 0.8 reduce_sum.22
  (1 shorter events, 0.0 us)
Async XLA Ops:
  0.6 76.2 %copy-start = (bf16[1,2048,512]{2,1,0:T(8,128)(2,1)S(1)}, bf16[1,2048,512]{2,1,0:T(8,128)(2,1)}, u32[]{:S(2)}) copy-start(bf16[1,2048,512]{2,1,0:T(8,128)(2,1)} %param.11) | copy-start | bytes 6291460
  76.7 1.6 %copy-start.1 = (bf16[1,2048,512]{2,1,0:T(8,128)(2,1)S(1)}, bf16[1,2048,512]{2,1,0:T(8,128)(2,1)}, u32[]{:S(2)}) copy-start(bf16[1,2048,512]{2,1,0:T(8,128)(2,1)} %param.12) | copy-start | bytes 6291460
  76.8 2.1 %copy-start.2 = (bf16[1,512,2048]{2,1,0:T(8,128)(2,1)S(1)}, bf16[1,512,2048]{2,1,0:T(8,128)(2,1)}, u32[]{:S(2)}) copy-start(bf16[1,512,2048]{2,1,0:T(8,128)(2,1)} %param.13) | copy-start | bytes 6291460
  82.2 13.3 %all-to-all-start = ((bf16[32,2,2048]{2,1,0:T(2,128)(2,1)}), bf16[32,2,2048]{2,1,0:T(2,128)(2,1)S(1)}, u32[]{:S(2)}, u32[]{:S(2)}) async-start(bf16[32,2,2048]{2,1,0:T(2,128)(2,1)} %reshape.14), calls=%async_computation | async-start | bytes 524288 | tf_op jit(solution)/shard_map/all_to_all | solution.py:51

commit v2 on v1

v2 whole, which is shorter than its diff:
```python
import functools

import jax
import jax.numpy as jnp
from jax import lax
from jax.experimental import pallas as pl
from jax.experimental.pallas import tpu as pltpu
from jax.sharding import PartitionSpec as P

LANES = 128
CORES = 2
BOTH = ("expert", "dp")
ROWS = 32
VMEM = pl.BlockSpec(memory_space=pltpu.VMEM)


def pack_kernel(tokens_ref, grad_ref, ids_ref, scores_ref, out_ref):
    chips, tok_dev, _ = out_ref.shape
    width = tokens_ref.shape[2]
    first = lax.axis_index("expert") * tok_dev
    ids = ids_ref[0]
    scores = scores_ref[0].astype(jnp.float32)
    token = lax.broadcasted_iota(jnp.int32, ids.shape, 1)
    lane = lax.broadcasted_iota(jnp.int32, (ids.shape[0], LANES), 1)
    row = lax.broadcasted_iota(jnp.int32, (tok_dev, LANES), 0)
    table = jnp.zeros((tok_dev, LANES), jnp.float32)
    for i in range(tok_dev):
        mine = token == first + i
        named = jnp.sum(jnp.where(mine, ids, 0), axis=1, keepdims=True)
        score = jnp.sum(jnp.where(mine, scores, 0.0), axis=1, keepdims=True)
        weights = jnp.sum(jnp.where(lane == named, score, 0.0), axis=0, keepdims=True)
        table = jnp.where(row == i, weights, table)
    table = table.astype(jnp.bfloat16)

    def write(chip, carry):
        out_ref[chip, :, :width] = tokens_ref[0]
        out_ref[chip, :, width : 2 * width] = grad_ref[0]
        out_ref[chip, :, 2 * width :] = table
        return carry

    lax.fori_loop(0, chips, write, 0, unroll=chips <= 16)


def pack(tokens, out_grad, expert_ids, gate_scores, chips):
    _, tok_dev, width = tokens.shape
    return pl.pallas_call(
        pack_kernel,
        out_shape=jax.ShapeDtypeStruct((chips, tok_dev, 2 * width + LANES), jnp.bfloat16),
        in_specs=[VMEM] * 4,
        out_specs=VMEM,
        compiler_params=pltpu.CompilerParams(vmem_limit_bytes=16 << 20),
    )(tokens, out_grad, jnp.swapaxes(expert_ids, 1, 2), jnp.swapaxes(gate_scores, 1, 2))


def rows_kernel(
    mine_ref, other_ref, gate_ref, up_ref, down_ref,
    shares_ref, x_ref, dy_ref, gate_delta_ref, up_delta_ref, hidden_ref,
):
    width = x_ref.shape[1]
    tok_dev = shares_ref.shape[1]
    my_expert = lax.axis_index("expert")
    my_core = lax.axis_index("dp") % CORES
    contract_last = (((1,), (1,)), ((), ()))
    devices = ROWS // tok_dev

    def step(block, carry):
        here = pl.ds(pl.multiple_of(block * ROWS, ROWS), ROWS)
        lane = lax.broadcasted_iota(jnp.int32, (ROWS, LANES), 1)
        x_parts, dy_parts = [], []
        for src in (mine_ref, other_ref):
            table = src[here, 2 * width :].astype(jnp.float32)
            weight = jnp.sum(jnp.where(lane == my_expert, table, 0.0), axis=1, keepdims=True)
            x_parts.append(src[here, :width])
            raw = src[here, width : 2 * width].astype(jnp.float32)
            dy_parts.append((raw * weight).astype(jnp.bfloat16))
        x = jnp.concatenate(x_parts, axis=0)
        dy = jnp.concatenate(dy_parts, axis=0)
        both = pl.ds(pl.multiple_of(block * 2 * ROWS, 2 * ROWS), 2 * ROWS)
        x_ref[both] = x
        dy_ref[both] = dy
        pre_gate = jnp.dot(x, gate_ref[0], preferred_element_type=jnp.float32)
        pre_up = jnp.dot(x, up_ref[0], preferred_element_type=jnp.float32)
        sigmoid_gate = jax.nn.sigmoid(pre_gate)
        activated = pre_gate * sigmoid_gate
        hidden_ref[both] = (activated * pre_up).astype(jnp.bfloat16)
        grad_hidden = lax.dot_general(
            dy, down_ref[0], contract_last, preferred_element_type=jnp.float32
        )
        gate_delta = (
            grad_hidden * pre_up * sigmoid_gate * (1.0 + pre_gate * (1.0 - sigmoid_gate))
        ).astype(jnp.bfloat16)
        up_delta = (grad_hidden * activated).astype(jnp.bfloat16)
        gate_delta_ref[both] = gate_delta
        up_delta_ref[both] = up_delta
        total = lax.dot_general(
            gate_delta, gate_ref[0], contract_last, preferred_element_type=jnp.float32
        )
        total = total + lax.dot_general(
            up_delta, up_ref[0], contract_last, preferred_element_type=jnp.float32
        )
        total = total.astype(jnp.bfloat16)
        for half, core in enumerate((my_core, 1 - my_core)):
            for j in range(devices):
                row = half * ROWS + j * tok_dev
                shares_ref[(block * devices + j) * CORES + core] = total[row : row + tok_dev]
        return carry

    blocks = mine_ref.shape[0] // ROWS
    if blocks == 1:
        step(0, 0)
    else:
        lax.fori_loop(0, blocks, step, 0)


def rows_pass(mine, other, w_gate, w_up, w_down, tok_dev):
    half, _ = mine.shape
    _, width, hidden = w_gate.shape
    rows = 2 * half
    bf16 = functools.partial(jax.ShapeDtypeStruct, dtype=jnp.bfloat16)
    weights = 3 * width * hidden * 2
    moved = weights + rows * (6 * width + 3 * hidden) * 2
    return pl.pallas_call(
        rows_kernel,
        out_shape=(
            bf16((rows // tok_dev, tok_dev, width)),
            bf16((rows, width)),
            bf16((rows, width)),
            bf16((rows, hidden)),
            bf16((rows, hidden)),
            bf16((rows, hidden)),
        ),
        in_specs=[VMEM] * 5,
        out_specs=(VMEM,) * 6,
        cost_estimate=pl.CostEstimate(
            flops=10 * rows * width * hidden, bytes_accessed=moved, transcendentals=rows * hidden
        ),
        compiler_params=pltpu.CompilerParams(vmem_limit_bytes=(12 << 20) + 2 * moved),
    )(mine, other, w_gate, w_up, w_down)


def local(tokens, out_grad, expert_ids, gate_scores, w_gate, w_up, w_down):
    tok_dev = tokens.shape[1]
    devices = lax.axis_size("expert") * lax.axis_size("dp")
    chips = devices // CORES
    same_core = [[chip * CORES + core for chip in range(chips)] for core in range(CORES)]
    core_pairs = [(d, d ^ 1) for d in range(devices)]
    copies = pack(tokens, out_grad, expert_ids, gate_scores, chips)
    mine = lax.all_to_all(copies, BOTH, 0, 0, axis_index_groups=same_core, tiled=True)
    other = lax.ppermute(mine, BOTH, core_pairs)
    half = chips * tok_dev
    shares, x, dy, gate_delta, up_delta, hidden = rows_pass(
        mine.reshape(half, -1), other.reshape(half, -1), w_gate, w_up, w_down, tok_dev
    )
    shares = lax.all_to_all(shares, BOTH, 0, 0, tiled=True)
    token_grad = jnp.sum(shares.astype(jnp.float32), axis=0)
    grad_down = jnp.dot(hidden.T, dy, preferred_element_type=jnp.float32)
    grad_gate = jnp.dot(x.T, gate_delta, preferred_element_type=jnp.float32)
    grad_up = jnp.dot(x.T, up_delta, preferred_element_type=jnp.float32)
    return tuple(g.astype(jnp.bfloat16)[None] for g in (token_grad, grad_gate, grad_up, grad_down))


def solution(mesh):
    return jax.shard_map(
        local,
        mesh=mesh,
        in_specs=(
            P("dp", "expert", None),
            P("dp", "expert", None),
            P("dp", None, None),
            P("dp", None, None),
            P("expert", None, "dp"),
            P("expert", None, "dp"),
            P("expert", "dp", None),
        ),
        out_specs=(
            P("dp", "expert", None),
            P("expert", None, "dp"),
            P("expert", None, "dp"),
            P("expert", "dp", None),
        ),
        check_vma=False,
    )
```

time: 96.6 us -> 45.7 us (0.47)
  blocking collectives: 72.8 us -> 18.1 us
  Pallas kernels: 0 us -> 3.6 us
  matrix products: 9.42 us -> 6.16 us
  local copies, waits for them, and re-layouts: 4.46 us -> 7.69 us
  waiting for transfers between devices: 4.5 us -> 5.56 us
    all_gather x1 -> x0, blocking collectives: 72.8 us -> none  [local(): rows = lax.all_gather(payload, BOTH, axis=0, tiled=True)]
    all_to_all x0 -> x1, blocking collectives: none -> 18.1 us  [local(): lax.all_to_all(copies, BOTH, 0, 0, axis_index_groups=same_core, tiled=True)]
    unnamed x7 -> x14, local copies, waits for them, and re-layouts: 1.38 us -> 7.49 us
    pallas_call x0 -> x2, Pallas kernels: none -> 3.6 us  [the longest x1 3.49 us: rows_pass(): pl.pallas_call(rows_kernel, out_shape=(bf16((rows // tok_dev, tok_dev, wi...]
    dot_general x5 -> x0, matrix products: 3.23 us -> none  [the longest x1 0.78 us: local(): grad_hidden = jnp.dot(dy, down_slab.T, preferred_element_type=jnp.float32)]
    dynamic_slice x4 -> x0, local copies, waits for them, and re-layouts: 1.83 us -> none  [the longest x2 0.98 us: pack(): lax.dynamic_slice_in_dim(gate_scores[0], my_expert * tok_dev, tok_dev, 0)]
    ppermute x0 -> x1, waiting for transfers between devices: none -> 1.44 us  [local(): other = lax.ppermute(mine, BOTH, core_pairs)]
  transfers between devices with their start and end apart: 1 -> 2, of which waited for: 1 -> 2; matrix products, arithmetic and copies ran while one was open for 6% -> 14% of each run, Pallas kernels for 0% -> 0%
where the time goes in v2:
time: 45.7 us; the launch traced here: 45.2 us
  blocking collectives  18.1 us (40%)
  local copies, waits for them, and re-layouts  7.69 us (17%)
  matrix products  6.16 us (13%)
  waiting for transfers between devices  5.56 us (12%)
  Pallas kernels  3.6 us (8%)
  starting transfers between devices  2.59 us (6%)
  other arithmetic  0.83 us (2%)
  between operations  0.68 us (1%)
    all_to_all x1, blocking collectives, local(): lax.all_to_all(copies, BOTH, 0, 0, axis_index_groups=same_core, tiled=True)  18.1 us
    unnamed x14, local copies, waits for them, and re-layouts  7.49 us
    all_to_all x1, waiting for transfers between devices, local(): shares = lax.all_to_all(shares, BOTH, 0, 0, tiled=True)  4.12 us
    pallas_call x1, Pallas kernels, rows_pass(): pl.pallas_call(rows_kernel, out_shape=(bf16((rows // tok_dev, tok_dev, wi...  3.49 us
    all_to_all x1, starting transfers between devices, local(): shares = lax.all_to_all(shares, BOTH, 0, 0, tiled=True)  2.58 us
    dot_general x1, matrix products, local(): grad_gate = jnp.dot(x.T, gate_delta, preferred_element_type=jnp.float32)  2.06 us
    dot_general x1, matrix products, local(): grad_up = jnp.dot(x.T, up_delta, preferred_element_type=jnp.float32)  2.05 us
    dot_general x1, matrix products, local(): grad_down = jnp.dot(hidden.T, dy, preferred_element_type=jnp.float32)  2.05 us
  transfers between devices with their start and end apart: 2, of which 2 were waited for; matrix products, arithmetic and copies ran while one was open for 14% of the time, Pallas kernels for 0%

profile of v2, /device:TPU:0, one launch (start us, length us, event | category | flops | bytes accessed | tf_op | source)
XLA Modules:
  0.0 45.2 jit_solution(12522534639643118088)
XLA Ops:
  0.6 0.0 copy-start.3
  0.6 0.7 %copy-done.3 = bf16[1,2,2048]{2,1,0:T(2,128)(2,1)S(1)} copy-done((bf16[1,2,2048]{2,1,0:T(2,128)(2,1)S(1)}, bf16[1,2,2048]{2,1,0:T(2,128)(2,1)}, u32[]{:S(2)}) %copy-start.3) | copy-done | bytes 8216
  1.3 0.0 copy-start.4
  1.3 0.7 %copy-done.4 = bf16[1,2,2048]{2,1,0:T(2,128)(2,1)S(1)} copy-done((bf16[1,2,2048]{2,1,0:T(2,128)(2,1)S(1)}, bf16[1,2,2048]{2,1,0:T(2,128)(2,1)}, u32[]{:S(2)}) %copy-start.4) | copy-done | bytes 8216
  2.0 0.0 copy-start.5
  2.0 0.7 %copy-done.5 = s32[1,4,2]{1,2,0:T(2,128)S(1)} copy-done((s32[1,4,2]{1,2,0:T(2,128)S(1)}, s32[1,4,2]{1,2,0:T(2,128)}, u32[]{:S(2)}) %copy-start.5) | copy-done | bytes 56
  2.7 0.0 copy-start.6
  2.7 0.7 %copy-done.6 = bf16[1,4,2]{1,2,0:T(2,128)(2,1)S(1)} copy-done((bf16[1,4,2]{1,2,0:T(2,128)(2,1)S(1)}, bf16[1,4,2]{1,2,0:T(2,128)(2,1)}, u32[]{:S(2)}) %copy-start.6) | copy-done | bytes 40
  3.4 0.1 shard_map.102
  3.5 18.1 %all_to_all.10 = bf16[16,2,4224]{2,1,0:T(2,128)(2,1)S(1)} all-to-all(bf16[16,2,4224]{2,1,0:T(2,128)(2,1)S(1)} %shard_map.102), channel_id=1, replica_groups={{0,2,4,6,8,10,12,14,16,18,20,22,24,26,28,30},{1,3,5,7,9,11,13,15,17,19,..., dimensions={0} | all-to-all | bytes 540672 | tf_op jit(solution)/shard_map/all_to_all | solution.py:148
  21.6 0.0 collective-permute-start
  21.6 0.1 reshape.14.mine_ref
  21.7 1.4 %collective-permute-done = bf16[16,2,4224]{2,1,0:T(2,128)(2,1)S(1)} collective-permute-done((bf16[16,2,4224]{2,1,0:T(2,128)(2,1)S(1)}, bf16[16,2,4224]{2,1,0:T(2,128)(2,1)S(1)}, u32[]{:S(2)}, u32[]{:S(2)}) %collective-permute-start) | collective-permute-done | bytes 270368 | tf_op jit(solution)/shard_map/ppermute | solution.py:149
  23.2 0.1 reshape.15.other_ref
  23.3 0.0 copy-start
  23.3 1.6 %copy-done = bf16[1,2048,512]{2,1,0:T(8,128)(2,1)S(1)} copy-done((bf16[1,2048,512]{2,1,0:T(8,128)(2,1)S(1)}, bf16[1,2048,512]{2,1,0:T(8,128)(2,1)}, u32[]{:S(2)}) %copy-start) | copy-done | bytes 2097176
  24.9 0.0 copy-start.1
  24.9 1.6 %copy-done.1 = bf16[1,2048,512]{2,1,0:T(8,128)(2,1)S(1)} copy-done((bf16[1,2048,512]{2,1,0:T(8,128)(2,1)S(1)}, bf16[1,2048,512]{2,1,0:T(8,128)(2,1)}, u32[]{:S(2)}) %copy-start.1) | copy-done | bytes 2097176
  26.5 0.0 copy-start.2
  26.5 1.6 %copy-done.2 = bf16[1,512,2048]{2,1,0:T(8,128)(2,1)S(1)} copy-done((bf16[1,512,2048]{2,1,0:T(8,128)(2,1)S(1)}, bf16[1,512,2048]{2,1,0:T(8,128)(2,1)}, u32[]{:S(2)}) %copy-start.2) | copy-done | bytes 2097176
  28.0 3.5 %shard_map.103 = (bf16[32,2,2048]{2,1,0:T(2,128)(2,1)}, bf16[64,2048]{1,0:T(8,128)(2,1)S(1)}, bf16[64,2048]{1,0:T(8,128)(2,1)S(1)}, bf16[64,512]{1,0:T(8,128)(2,...) custom-call(bf16[32,4224]{1,0:T(8,128)(2,1)S(1)} %reshape.14.mine_ref, ...), custom_call_target="tpu_custom_call" | custom-call | flops 671088640 | bytes 8060928 | tf_op jit(solution)/shard_map/pallas_call | solution.py:122
  31.5 2.6 %all-to-all-start.1 = ((bf16[32,2,2048]{2,1,0:T(2,128)(2,1)}), bf16[32,2,2048]{2,1,0:T(2,128)(2,1)S(1)}, u32[]{:S(2)}, u32[]{:S(2)}) async-start(bf16[32,2,2048]{2,1,0:T(2,128)(2,1)} %get-tuple-element.10), calls=%async_computation.1 | async-start | bytes 524288 | tf_op jit(solution)/shard_map/all_to_all | solution.py:154
  34.1 2.1 %fusion = bf16[1,2048,512]{2,1,0:T(8,128)(2,1)} fusion(bf16[64,2048]{1,0:T(8,128)(2,1)S(1)} %get-tuple-element.11, bf16[64,512]{1,0:T(8,128)(2,1)S(1)} %get-tuple-element.12), kind=kOutput, calls=%fused_computation.3 | convolution fusion | flops 135266304 | bytes 2424832 | tf_op jit(solution)/shard_map/dot_general | solution.py:157
  36.2 2.1 %fusion.1 = bf16[1,2048,512]{2,1,0:T(8,128)(2,1)} fusion(bf16[64,2048]{1,0:T(8,128)(2,1)S(1)} %get-tuple-element.11, bf16[64,512]{1,0:T(8,128)(2,1)S(1)} %get-tuple-element.13), kind=kOutput, calls=%fused_computation.4 | convolution fusion | flops 135266304 | bytes 2424832 | tf_op jit(solution)/shard_map/dot_general | solution.py:158
  38.2 2.0 %fusion.2 = bf16[1,512,2048]{2,1,0:T(8,128)(2,1)} fusion(bf16[64,512]{1,0:T(8,128)(2,1)S(1)} %get-tuple-element.14, bf16[64,2048]{1,0:T(8,128)(2,1)S(1)} %get-tuple-element.15), kind=kOutput, calls=%fused_computation.5 | convolution fusion | flops 135266304 | bytes 2424832 | tf_op jit(solution)/shard_map/dot_general | solution.py:156
  40.3 4.1 %all-to-all-done.1 = bf16[32,2,2048]{2,1,0:T(2,128)(2,1)S(1)} async-done(((bf16[32,2,2048]{2,1,0:T(2,128)(2,1)}), bf16[32,2,2048]{2,1,0:T(2,128)(2,1)S(1)}, u32[]{:S(2)}, u32[]{:S(2)}) %all-to-all-start.1) | async-done | bytes 262176 | tf_op jit(solution)/shard_map/all_to_all | solution.py:154
  44.4 0.8 %reduce_sum.12 = bf16[2,2048]{1,0:T(2,128)(2,1)} reduce(bf16[32,2,2048]{2,1,0:T(2,128)(2,1)S(1)} %all-to-all-done.1, bf16[]{:T(256)} %constant.2.clone.1), dimensions={0}, to_apply=%region_0.0 | reduce | flops 126976 | bytes 270338 | tf_op jit(solution)/shard_map/reduce_sum | solution.py:155
Async XLA Ops:
  0.6 0.7 %copy-start.3 = (bf16[1,2,2048]{2,1,0:T(2,128)(2,1)S(1)}, bf16[1,2,2048]{2,1,0:T(2,128)(2,1)}, u32[]{:S(2)}) copy-start(bf16[1,2,2048]{2,1,0:T(2,128)(2,1)} %tokens_ref.1) | copy-start | bytes 24580
  1.3 0.7 %copy-start.4 = (bf16[1,2,2048]{2,1,0:T(2,128)(2,1)S(1)}, bf16[1,2,2048]{2,1,0:T(2,128)(2,1)}, u32[]{:S(2)}) copy-start(bf16[1,2,2048]{2,1,0:T(2,128)(2,1)} %grad_ref.1) | copy-start | bytes 24580
  2.0 0.7 %copy-start.5 = (s32[1,4,2]{1,2,0:T(2,128)S(1)}, s32[1,4,2]{1,2,0:T(2,128)}, u32[]{:S(2)}) copy-start(s32[1,4,2]{1,2,0:T(2,128)} %param.9) | copy-start | bytes 100
  2.7 0.7 %copy-start.6 = (bf16[1,4,2]{1,2,0:T(2,128)(2,1)S(1)}, bf16[1,4,2]{1,2,0:T(2,128)(2,1)}, u32[]{:S(2)}) copy-start(bf16[1,4,2]{1,2,0:T(2,128)(2,1)} %param.10) | copy-start | bytes 52
  21.6 1.5 %collective-permute-start = (bf16[16,2,4224]{2,1,0:T(2,128)(2,1)S(1)}, bf16[16,2,4224]{2,1,0:T(2,128)(2,1)S(1)}, u32[]{:S(2)}, u32[]{:S(2)}) collective-permute-start(bf16[16,2,4224]{2,1,0:T(2,128)(2,1)S(1)} %all_to_all.10), channel_id=1, source_target_pairs={{0,1},{1,0},{2,3},{3,2},{4,5},{5,4},{6,7},{7,6},{8,9},{9,8},{10,11... | collective-permute-start | bytes 811016 | tf_op jit(solution)/shard_map/ppermute | solution.py:149
  23.3 1.6 %copy-start = (bf16[1,2048,512]{2,1,0:T(8,128)(2,1)S(1)}, bf16[1,2048,512]{2,1,0:T(8,128)(2,1)}, u32[]{:S(2)}) copy-start(bf16[1,2048,512]{2,1,0:T(8,128)(2,1)} %gate_ref.1) | copy-start | bytes 6291460
  24.9 1.6 %copy-start.1 = (bf16[1,2048,512]{2,1,0:T(8,128)(2,1)S(1)}, bf16[1,2048,512]{2,1,0:T(8,128)(2,1)}, u32[]{:S(2)}) copy-start(bf16[1,2048,512]{2,1,0:T(8,128)(2,1)} %up_ref.1) | copy-start | bytes 6291460
  26.5 1.6 %copy-start.2 = (bf16[1,512,2048]{2,1,0:T(8,128)(2,1)S(1)}, bf16[1,512,2048]{2,1,0:T(8,128)(2,1)}, u32[]{:S(2)}) copy-start(bf16[1,512,2048]{2,1,0:T(8,128)(2,1)} %down_ref.1) | copy-start | bytes 6291460
  31.5 12.9 %all-to-all-start.1 = ((bf16[32,2,2048]{2,1,0:T(2,128)(2,1)}), bf16[32,2,2048]{2,1,0:T(2,128)(2,1)S(1)}, u32[]{:S(2)}, u32[]{:S(2)}) async-start(bf16[32,2,2048]{2,1,0:T(2,128)(2,1)} %get-tuple-element.10), calls=%async_computation.1 | async-start | bytes 524288 | tf_op jit(solution)/shard_map/all_to_all | solution.py:154
